TPU v7x, 32 devices: a whole 2x2x4 slice. The times are simulated.
32 devices in a mesh: segment: 4 (over y, x), fsdp: 4 (over z), rep: 2 (over core).
Axes of the slice: x: 2, y: 2, z: 4, core: 2. Of those that a mesh axis runs over, the one named last changes fastest.
Arguments:
- token_ids: int32 [32, 128], P('fsdp'), may hold values from 0 to 127
- seq_lengths: int32 [32], P('fsdp'), may hold values from 32 to 128, as said below
- quant_scores: int32 [32], P('fsdp'), may hold values from 0 to 64
- embed_table: bfloat16 [128, 4096], replicated, may hold values from -6 to 6
- prior_weight: bfloat16 [4, 4096, 4096], P('segment', None, 'rep'), may hold values from -0.09375 to 0.09375
- prior_gain: float32 [4, 4096], P('segment'), may hold values from 0.25 to 1.75
- final_gain: float32 [4096], replicated, may hold values from 0.25 to 1.75
- head_weight: bfloat16 [4096, 128], replicated, may hold values from -0.25 to 0.25
- agent_down: bfloat16 [4096, 256], P('fsdp'), may hold values from -0.09375 to 0.09375
- agent_up: bfloat16 [4096, 256], P('fsdp'), may hold values from -0.375 to 0.375
Outputs:
- down_gradient: float32 [4096, 256], P(('segment', 'fsdp', 'rep'))
- up_gradient: float32 [4096, 256], P(('segment', 'fsdp', 'rep'))
Inputs may be any that keep to these rules, and one draw needn't show every extreme that they name: `seq_lengths`: every sequence keeps at least 32 tokens, and some sequence in every draw has all 128.
All inputs are finite; a program needn't handle non-finite values.
Results may differ from a plain program's by a relative error of at most 0.0081.
Values may be sent and summed in bfloat16 or wider, within the bound.
A program may use at most 128 MiB of HBM per device.

v0:
```python
import jax
import jax.numpy as jnp
from jax import lax
from jax.sharding import PartitionSpec as P

LEVELS = 64
EPSILON = 1e-05
SIGMA_WEIGHT = 2.0

bf16 = jnp.bfloat16
f32 = jnp.float32


def rms_scale(values):
    squares = jnp.mean(values * values, axis=-1, keepdims=True)
    return lax.rsqrt(squares + EPSILON)


def dot(a, b, dims):
    return lax.dot_general(a, b, (dims, ((), ())), preferred_element_type=f32)


def on_device(
    token_ids,
    seq_lengths,
    quant_scores,
    embed_table,
    prior_weight,
    prior_gain,
    final_gain,
    head_weight,
    agent_down,
    agent_up,
):
    segments = lax.axis_size("segment")
    groups = lax.axis_size("fsdp")
    replicas = lax.axis_size("rep")
    segment_pos = lax.axis_index("segment")
    group_pos = lax.axis_index("fsdp")
    rep_pos = lax.axis_index("rep")
    vocab, width = embed_table.shape
    half = prior_weight.shape[2]
    seq_len = token_ids.shape[1]
    weight = prior_weight[0]
    gain = prior_gain[0]
    own_rows = vocab // groups

    rows = lax.dynamic_slice_in_dim(embed_table, group_pos * own_rows, own_rows, 0)
    pairs = [(i, i + 1) for i in range(segments - 1)]
    for s in range(segments):
        wide = rows.astype(f32)
        normed = (wide * rms_scale(wide) * gain).astype(bf16)
        update = dot(normed, weight, ((1,), (0,)))
        own = lax.dynamic_slice_in_dim(wide, rep_pos * half, half, 1)
        part = (own + update).astype(bf16)
        rows = lax.all_gather(part, "rep", axis=1, tiled=True)
        if s < segments - 1:
            rows = lax.ppermute(rows, "segment", pairs)
    wide = rows.astype(f32)
    prior_final = (wide * rms_scale(wide) * final_gain).astype(bf16)
    prior_part = jax.nn.log_softmax(dot(prior_final, head_weight, ((1,), (0,))), axis=-1)
    prior_part = jnp.where(segment_pos == segments - 1, prior_part, 0.0)
    slot = jnp.zeros((vocab, vocab), f32)
    slot = lax.dynamic_update_slice_in_dim(slot, prior_part, group_pos * own_rows, 0)
    prior_logp = lax.psum(slot, ("segment", "fsdp"))

    ids = lax.all_gather(token_ids, "fsdp", axis=0, tiled=True)
    lengths = lax.all_gather(seq_lengths, "fsdp", axis=0, tiled=True)
    scores = lax.all_gather(quant_scores, "fsdp", axis=0, tiled=True)
    down = lax.all_gather(agent_down, "fsdp", axis=0, tiled=True)
    up = lax.all_gather(agent_up, "fsdp", axis=0, tiled=True)
    start = embed_table.astype(f32)
    unit = (start * rms_scale(start)).astype(bf16)
    latent = dot(unit, down, ((1,), (0,))).astype(bf16)
    hidden = start + dot(latent, up, ((1,), (1,)))
    inverse = rms_scale(hidden)
    agent_final = (hidden * inverse * final_gain).astype(bf16)
    agent_logp = jax.nn.log_softmax(dot(agent_final, head_weight, ((1,), (0,))), axis=-1)

    seqs = ids.shape[0]
    next_ids = jnp.concatenate([ids[:, 1:], ids[:, :1]], axis=1)
    live = (jnp.arange(seq_len, dtype=jnp.int32)[None, :] < lengths[:, None] - 1)
    counts = (lengths - 1).astype(f32)
    column = jnp.arange(vocab, dtype=jnp.int32)
    here = (ids.reshape(-1)[:, None] == column).astype(bf16)
    there = (next_ids.reshape(-1)[:, None] == column) & live.reshape(-1)[:, None]
    gap = prior_logp - agent_logp
    gap_hi = gap.astype(bf16)
    gap_lo = (gap - gap_hi.astype(f32)).astype(bf16)
    looked = dot(here, gap_hi, ((1,), (0,))) + dot(here, gap_lo, ((1,), (0,)))
    term = jnp.sum(jnp.where(there, looked, 0.0).reshape(seqs, seq_len * vocab), axis=1)
    margin = term / counts + SIGMA_WEIGHT * scores.astype(f32) / LEVELS
    factor = 2.0 * margin / counts

    token_factor = jnp.repeat(factor, seq_len)
    weighted = jnp.where(there, token_factor[:, None], 0.0)
    weighted_hi = weighted.astype(bf16)
    weighted_lo = (weighted - weighted_hi.astype(f32)).astype(bf16)
    pair_sum = dot(here, weighted_hi, ((0,), (0,))) + dot(here, weighted_lo, ((0,), (0,)))
    logit_grad = jnp.sum(pair_sum, axis=1, keepdims=True) * jnp.exp(agent_logp) - pair_sum
    scaled = dot(logit_grad.astype(bf16), head_weight, ((1,), (1,))) * final_gain
    hidden_grad = (
        inverse * scaled
        - hidden * inverse * inverse * inverse * jnp.mean(hidden * scaled, axis=-1, keepdims=True)
    ).astype(bf16)
    latent_grad = dot(hidden_grad, up, ((1,), (0,))).astype(bf16)
    share = width // (segments * groups * replicas)
    first = ((segment_pos * groups + group_pos) * replicas + rep_pos) * share
    own_unit = lax.dynamic_slice_in_dim(unit, first, share, 1)
    own_grad = lax.dynamic_slice_in_dim(hidden_grad, first, share, 1)
    return (
        dot(own_unit, latent_grad, ((0,), (0,))),
        dot(own_grad, latent, ((0,), (0,))),
    )


def solution(mesh):
    placed = (
        P("fsdp", None),
        P("fsdp"),
        P("fsdp"),
        P(),
        P("segment", None, "rep"),
        P("segment", None),
        P(),
        P(),
        P("fsdp", None),
        P("fsdp", None),
    )
    spread = P(("segment", "fsdp", "rep"), None)
    return jax.shard_map(
        on_device, mesh=mesh, in_specs=placed, out_specs=(spread, spread), check_vma=False
    )
```

profile of v0, /device:TPU:0, one launch (start us, length us, event | category | flops | bytes accessed | tf_op | source)
XLA Modules:
  0.0 226.8 jit_solution(13667713728466787973)
XLA Ops:
  8.8 1.1 multiply_reduce_fusion.5
  9.9 1.0 dynamic-slice_convert_fusion
  10.9 9.0 %fusion.12 = bf16[32,2048]{1,0:T(8,128)(2,1)S(1)} fusion(bf16[1,4096,2048]{2,1,0:T(8,128)(2,1)} %param.14, f32[32,4096]{1,0:T(8,128)S(1)} %dynamic-slice_convert_fusion, f32[4096]{0:T(1024)} %bitcast.41, f32[32]{0:T(128)S(1)} %add_rsqrt_fusion.4, s32[]{:T(128)S(6)} %select_n.33), kind=kOutput, calls=%fused_computation.17 | convolution fusion | flops 537395200 | bytes 17711620 | tf_op jit(solution)/shard_map/dot_general | solution.py:20
  19.9 2.1 all_gather.31
  22.0 4.8 %collective-permute-start = (bf16[32,4096]{1,0:T(8,128)(2,1)S(1)}, bf16[32,4096]{1,0:T(8,128)(2,1)S(1)}, u32[]{:S(2)}, u32[]{:S(2)}) collective-permute-start(bf16[32,4096]{1,0:T(8,128)(2,1)S(1)} %all_gather.31), channel_id=1, source_target_pairs={{0,8},{8,16},{16,24},{1,9},{9,17},{17,25},{2,10},{10,18},{18,26},{... | collective-permute-start | bytes 786440 | tf_op jit(solution)/shard_map/ppermute | solution.py:58
  27.1 5.5 %collective-permute-done = bf16[32,4096]{1,0:T(8,128)(2,1)S(1)} collective-permute-done((bf16[32,4096]{1,0:T(8,128)(2,1)S(1)}, bf16[32,4096]{1,0:T(8,128)(2,1)S(1)}, u32[]{:S(2)}, u32[]{:S(2)}) %collective-permute-start) | collective-permute-done | bytes 262176 | tf_op jit(solution)/shard_map/ppermute | solution.py:58
  32.8 8.9 %add_convert_fusion.2 = bf16[32,2048]{1,0:T(8,128)(2,1)S(1)} fusion(f32[32,4096]{1,0:T(8,128)S(1)} %convert_element_type.94, s32[]{:T(128)S(6)} %select_n.33, bf16[1,4096,2048]{2,1,0:T(8,128)(2,1)} %param.14, f32[32]{0:T(128)S(1)} %add_rsqrt_fusion.3, bf16[32,4096]{1,0:T(8,128)(2,1)S(1)} %collective-permute-done, f32[4096]{0:T(1024)S(1)} %bitcast.42), kind=kOutput, calls=%fused_computation.73 | convolution fusion | flops 537526272 | bytes 17449092 | tf_op jit(solution)/shard_map/dot_general | solution.py:20
  41.8 2.3 all_gather.32
  44.1 4.4 %collective-permute-start.1 = (bf16[32,4096]{1,0:T(8,128)(2,1)}, bf16[32,4096]{1,0:T(8,128)(2,1)S(1)}, u32[]{:S(2)}, u32[]{:S(2)}) collective-permute-start(bf16[32,4096]{1,0:T(8,128)(2,1)} %all_gather.32), channel_id=1, source_target_pairs={{0,8},{8,16},{16,24},{1,9},{9,17},{17,25},{2,10},{10,18},{18,26},{... | collective-permute-start | bytes 786440 | tf_op jit(solution)/shard_map/ppermute | solution.py:58
  48.8 13.4 %all_gather.29 = s32[32,128]{1,0:T(8,128)S(1)} all-gather(s32[8,128]{1,0:T(8,128)S(1)} %copy-done.8), channel_id=1, replica_groups=mesh['segment'=4,'fsdp'=4,'rep'=2] {'fsdp'}, dimensions={0}, use_global_device_ids=true | all-gather | bytes 20480 | tf_op jit(solution)/shard_map/all_gather | solution.py:67
  64.0 8.0 %all-reduce.2 = (s32[32]{0:T(128)S(1)}, s32[32]{0:T(128)S(1)}) all-reduce(s32[32]{0:T(128)S(1)} %dynamic-update-slice.1, s32[32]{0:T(128)S(1)} %dynamic-update-slice), channel_id=1, replica_groups=mesh['segment'=4,'fsdp'=4,'rep'=2] {'fsdp'}, use_global_device_ids=true, to_apply=%add.1 | all-reduce | flops 64 | bytes 512
  72.2 8.9 %add_convert_fusion.1 = bf16[32,2048]{1,0:T(8,128)(2,1)S(1)} fusion(f32[32,4096]{1,0:T(8,128)S(1)} %convert_element_type.97, s32[]{:T(128)S(6)} %select_n.33, bf16[1,4096,2048]{2,1,0:T(8,128)(2,1)} %param.14, f32[32]{0:T(128)S(1)} %add_rsqrt_fusion.2, bf16[32,4096]{1,0:T(8,128)(2,1)S(1)} %collective-permute-done.1, f32[4096]{0:T(1024)S(1)} %bitcast.43), kind=kOutput, calls=%fused_computation.70 | convolution fusion | flops 537526272 | bytes 17449092 | tf_op jit(solution)/shard_map/dot_general | solution.py:20
  81.1 2.0 all_gather.33
  83.1 5.0 %collective-permute-start.2 = (bf16[32,4096]{1,0:T(8,128)(2,1)S(1)}, bf16[32,4096]{1,0:T(8,128)(2,1)S(1)}, u32[]{:S(2)}, u32[]{:S(2)}) collective-permute-start(bf16[32,4096]{1,0:T(8,128)(2,1)S(1)} %all_gather.33), channel_id=1, source_target_pairs={{0,8},{8,16},{16,24},{1,9},{9,17},{17,25},{2,10},{10,18},{18,26},{... | collective-permute-start | bytes 786440 | tf_op jit(solution)/shard_map/ppermute | solution.py:58
  88.2 5.5 %collective-permute-done.2 = bf16[32,4096]{1,0:T(8,128)(2,1)S(1)} collective-permute-done((bf16[32,4096]{1,0:T(8,128)(2,1)S(1)}, bf16[32,4096]{1,0:T(8,128)(2,1)S(1)}, u32[]{:S(2)}, u32[]{:S(2)}) %collective-permute-start.2) | collective-permute-done | bytes 262176 | tf_op jit(solution)/shard_map/ppermute | solution.py:58
  94.0 8.9 %add_convert_fusion = bf16[32,2048]{1,0:T(8,128)(2,1)S(1)} fusion(f32[32,4096]{1,0:T(8,128)S(1)} %convert_element_type.100, s32[]{:T(128)S(6)} %select_n.33, bf16[1,4096,2048]{2,1,0:T(8,128)(2,1)} %param.14, f32[32]{0:T(128)S(1)} %add_rsqrt_fusion.1, bf16[32,4096]{1,0:T(8,128)(2,1)S(1)} %collective-permute-done.2, f32[4096]{0:T(1024)S(1)} %bitcast.44), kind=kOutput, calls=%fused_computation.67 | convolution fusion | flops 537526272 | bytes 17449092 | tf_op jit(solution)/shard_map/dot_general | solution.py:20
  102.8 2.0 all_gather.34
  107.0 2.0 convolution_convert_fusion.1
  109.1 2.8 %multiply_reduce_fusion.1 = (f32[128]{0:T(128)S(1)}, f32[128,4096]{1,0:T(8,128)S(1)}) fusion(bf16[128,256]{1,0:T(8,128)(2,1)S(1)} %convolution_convert_fusion.1, bf16[4096,256]{1,0:T(8,128)(2,1)} %all-gather.5.cloned.1.call-done, bf16[128,4096]{1,0:T(8,128)(2,1)} %param.13), kind=kOutput, calls=%fused_computation.29 | convolution fusion | flops 270532480 | bytes 5308928 | tf_op jit(solution)/shard_map/dot_general | solution.py:20
  112.5 95.5 %all-reduce.5.cloned.1.call-done = f32[128,128]{0,1:T(8,128)} async-done(((f32[128,128]{0,1:T(8,128)}), f32[128,128]{0,1:T(8,128)}) %all-reduce.5.cloned.1.call-update) | async-done | bytes 65552 | tf_op jit(solution)/shard_map/psum | solution.py:65
  208.0 1.8 fusion.20
  209.8 1.2 fusion.22
  212.1 1.0 fusion.81
  216.2 3.2 %fusion.23 = f32[128,256]{1,0:T(8,128)} fusion(bf16[128,4096]{1,0:T(8,128)(2,1)} %copy-done.3, bf16[4096,256]{1,0:T(8,128)(2,1)} %all-gather.5.cloned.1.call-done, bf16[128,4096]{1,0:T(8,128)(2,1)} %copy-done.2, s32[]{:T(128)S(6)} %select_n.30), kind=kOutput, calls=%fused_computation.34 | convolution fusion | flops 276856832 | bytes 3309572 | tf_op jit(solution)/shard_map/dot_general | solution.py:20
  (76 shorter events, 10.2 us)
Async XLA Ops:
  8.0 97.0 %copy-start = (bf16[4096,128]{1,0:T(8,128)(2,1)S(1)}, bf16[4096,128]{1,0:T(8,128)(2,1)}, u32[]{:S(2)}) copy-start(bf16[4096,128]{1,0:T(8,128)(2,1)} %param.17) | copy-start | bytes 3145732
  8.0 99.0 %all-gather.3.cloned.1.call-start = ((), (), s32[]{:S(2)}) async-start(), calls=%async_computation | async-start | bytes 2621440 | tf_op jit(solution)/shard_map/all_gather | solution.py:70
  8.7 100.3 %all-gather.5.cloned.1.call-start = ((), (), s32[]{:S(2)}) async-start(), calls=%async_computation.1 | async-start | bytes 2621440 | tf_op jit(solution)/shard_map/all_gather | solution.py:71
  10.9 15.9 %copy-start.1 = (bf16[128,4096]{1,0:T(8,128)(2,1)S(1)}, bf16[128,4096]{1,0:T(8,128)(2,1)}, u32[]{:S(2)}) copy-start(bf16[128,4096]{1,0:T(8,128)(2,1)} %param.13) | copy-start | bytes 3145732
  19.9 12.9 %copy-start.4 = (f32[1,4096]{1,0:T(1,128)S(1)}, f32[1,4096]{1,0:T(1,128)}, u32[]{:S(2)}) copy-start(f32[1,4096]{1,0:T(1,128)} %param.15) | copy-start | bytes 49156
  22.0 10.6 %collective-permute-start = (bf16[32,4096]{1,0:T(8,128)(2,1)S(1)}, bf16[32,4096]{1,0:T(8,128)(2,1)S(1)}, u32[]{:S(2)}, u32[]{:S(2)}) collective-permute-start(bf16[32,4096]{1,0:T(8,128)(2,1)S(1)} %all_gather.31), channel_id=1, source_target_pairs={{0,8},{8,16},{16,24},{1,9},{9,17},{17,25},{2,10},{10,18},{18,26},{... | collective-permute-start | bytes 786440 | tf_op jit(solution)/shard_map/ppermute | solution.py:58
  26.8 181.2 %all-reduce.5.cloned.1.call-start = ((), (), s32[]{:S(2)}) async-start(), calls=%async_computation.2 | async-start | bytes 131072 | tf_op jit(solution)/shard_map/psum | solution.py:65
  41.8 7.0 %copy-start.8 = (s32[8,128]{1,0:T(8,128)S(1)}, s32[8,128]{1,0:T(8,128)}, u32[]{:S(2)}) copy-start(s32[8,128]{1,0:T(8,128)} %param.10) | copy-start | bytes 12292
  41.8 20.5 %copy-start.11 = (u32[32]{0:T(128)S(1)}, u32[32]{0:T(128)}, u32[]{:S(2)}) copy-start(u32[32]{0:T(128)} %constant.72) | copy-start | bytes 388
  41.8 21.7 %copy-start.9 = (s32[8]{0:T(128)S(1)}, s32[8]{0:T(128)}, u32[]{:S(2)}) copy-start(s32[8]{0:T(128)} %param.12) | copy-start | bytes 100
  41.8 21.9 %copy-start.10 = (s32[8]{0:T(128)S(1)}, s32[8]{0:T(128)}, u32[]{:S(2)}) copy-start(s32[8]{0:T(128)} %param.11) | copy-start | bytes 100
  44.1 27.9 %collective-permute-start.1 = (bf16[32,4096]{1,0:T(8,128)(2,1)}, bf16[32,4096]{1,0:T(8,128)(2,1)S(1)}, u32[]{:S(2)}, u32[]{:S(2)}) collective-permute-start(bf16[32,4096]{1,0:T(8,128)(2,1)} %all_gather.32), channel_id=1, source_target_pairs={{0,8},{8,16},{16,24},{1,9},{9,17},{17,25},{2,10},{10,18},{18,26},{... | collective-permute-start | bytes 786440 | tf_op jit(solution)/shard_map/ppermute | solution.py:58
  48.7 58.3 %copy-start.2 = (bf16[128,4096]{1,0:T(8,128)(2,1)}, bf16[128,4096]{1,0:T(8,128)(2,1)S(1)}, u32[]{:S(2)}) copy-start(bf16[128,4096]{1,0:T(8,128)(2,1)S(1)} %fusion.17) | copy-start | bytes 3145732
  83.1 10.7 %collective-permute-start.2 = (bf16[32,4096]{1,0:T(8,128)(2,1)S(1)}, bf16[32,4096]{1,0:T(8,128)(2,1)S(1)}, u32[]{:S(2)}, u32[]{:S(2)}) collective-permute-start(bf16[32,4096]{1,0:T(8,128)(2,1)S(1)} %all_gather.33), channel_id=1, source_target_pairs={{0,8},{8,16},{16,24},{1,9},{9,17},{17,25},{2,10},{10,18},{18,26},{... | collective-permute-start | bytes 786440 | tf_op jit(solution)/shard_map/ppermute | solution.py:58
  94.0 11.1 %copy-start.6 = (f32[4096]{0:T(1024)S(1)}, f32[4096]{0:T(1024)}, u32[]{:S(2)}) copy-start(f32[4096]{0:T(1024)} %param.16) | copy-start | bytes 49156
  106.3 0.6 copy-start.5
  208.0 1.8 copy-start.7
  214.3 1.0 copy-start.3
Sparse Core Ops, SparseCore 0:
  10.4 48.7 all-gather.2
  60.8 45.1 all-gather.4
Sparse Core Ops, SparseCore 1:
  107.0 100.9 all-reduce.4
where the time goes:
time: 227 us
  waiting for transfers between devices  107 us (47%)
  matrix products  51 us (22%)
  blocking collectives  29.7 us (13%)
  between operations  16.5 us (7%)
  starting transfers between devices  14.3 us (6%)
  other arithmetic  4.68 us (2%)
  local copies, waits for them, and re-layouts  3.38 us (1%)
    psum x1, waiting for transfers between devices, on_device(): prior_logp = lax.psum(slot, ('segment', 'fsdp'))  95.5 us
    dot_general x15, matrix products, dot(): return lax.dot_general(a, b, (dims, ((), ())), preferred_element_type=f32)  51 us
    ppermute x3, starting transfers between devices, on_device(): rows = lax.ppermute(rows, 'segment', pairs)  14.2 us
    all_gather x1, blocking collectives, on_device(): ids = lax.all_gather(token_ids, 'fsdp', axis=0, tiled=True)  13.4 us
    ppermute x3, waiting for transfers between devices, on_device(): rows = lax.ppermute(rows, 'segment', pairs)  11 us
    all_gather x4, blocking collectives, on_device(): rows = lax.all_gather(part, 'rep', axis=1, tiled=True)  8.33 us
    unnamed x1, blocking collectives  7.98 us
  transfers between devices with their start and end apart: 6, of which 3 were waited for; matrix products, arithmetic and copies ran while one was open for 21% of the time, Pallas kernels for 0%

commit v1 on v0

v1 whole, which is shorter than its diff:
```python
import functools

import jax
import jax.numpy as jnp
from jax import lax
from jax.experimental import pallas as pl
from jax.experimental.pallas import tpu as pltpu
from jax.sharding import PartitionSpec as P

LEVELS = 64
EPSILON = 1e-05
SIGMA_WEIGHT = 2.0
MESH = pl.DeviceIdType.MESH

bf16 = jnp.bfloat16
f32 = jnp.float32
CHUNK = 256


def dot(a, b, dims=((1,), (0,)), precision=None):
    return lax.dot_general(a, b, (dims, ((), ())), precision=precision, preferred_element_type=f32)


def exact(a, b, dims=((1,), (0,))):
    return dot(a, b, dims, lax.Precision.HIGHEST)


def halves(a):
    high = a.astype(bf16)
    return high, (a - high.astype(f32)).astype(bf16)


def log_softmax(logits):
    shifted = logits - jnp.max(logits, axis=-1, keepdims=True)
    return shifted - jnp.log(jnp.sum(jnp.exp(shifted), axis=-1, keepdims=True))


def kernel(
    sizes,
    pack_ref,
    embed_ref,
    gain_ref,
    final_gain_ref,
    head_ref,
    down_ref,
    up_ref,
    embed_share_ref,
    head_share_ref,
    gain_share_ref,
    weight_hbm,
    down_out,
    up_out,
    weight,
    x_buf,
    normed,
    out_buf,
    tokens,
    part,
    from_z,
    gathered,
    up_share,
    pair_count,
    exchange,
    terms,
    factor_buf,
    lat_buf,
    wide_buf,
    rank_buf,
    agent_terms,
    hidden_share,
    weight_sem,
    x_send,
    x_recv,
    tok_send,
    tok_recv,
    z_send,
    z_recv,
    g_send,
    g_recv,
    u_send,
    u_recv,
    e_send,
    e_recv,
    t_send,
    t_recv,
):
    S, G, R = sizes
    seg, grp, rep = lax.axis_index("segment"), lax.axis_index("fsdp"), lax.axis_index("rep")
    vocab, width = embed_ref.shape
    rank = up_ref.shape[1]
    depth = up_ref.shape[0]
    rows = x_buf.shape[1]
    blocks = vocab // rows
    cohort = grp // blocks
    block = grp - cohort * blocks
    chunks = out_buf.shape[0]
    teams = S * R
    team = seg * R + rep
    vr, rr = vocab // teams, rank // teams
    share = up_share.shape[0]
    seqs = pair_count.shape[0]
    group_seqs = seqs // G

    def remote(src, dst, send, recv, device):
        return pltpu.make_async_remote_copy(
            src_ref=src, dst_ref=dst, send_sem=send, recv_sem=recv, device_id=device, device_id_type=MESH
        )

    def weight_copy(j):
        cols = pl.ds(pl.multiple_of(j * CHUNK, CHUNK), CHUNK)
        return pltpu.make_async_copy(weight_hbm.at[0, :, cols], weight.at[j], weight_sem.at[j])

    def start_weight(j, carry):
        weight_copy(j).start()
        return carry

    lax.fori_loop(0, chunks, start_weight, 0)

    barrier = pltpu.get_barrier_semaphore()
    for a in range(S):
        for b in range(G):
            for c in range(R):
                if a + b + c:
                    other = (lax.rem(seg + a, S), lax.rem(grp + b, G), lax.rem(rep + c, R))
                    pl.semaphore_signal(barrier, inc=1, device_id=other, device_id_type=MESH)
    pl.semaphore_wait(barrier, S * G * R - 1)

    tokens[grp] = pack_ref[...]
    token_copies = [
        remote(
            pack_ref, tokens.at[grp], tok_send.at[b - 1], tok_recv.at[b - 1], (seg, lax.rem(grp + b, G), rep)
        )
        for b in range(1, G)
    ]
    for copy in token_copies:
        copy.start()

    def x_copy(j, to):
        return remote(
            out_buf.at[j],
            x_buf.at[rep * chunks + j],
            x_send.at[j, to],
            x_recv.at[rep * chunks + j],
            (lax.rem(seg + 1, S), grp, to),
        )

    def x_arrival(c):
        return remote(out_buf.at[0], x_buf.at[c], x_send.at[0, 0], x_recv.at[c], (lax.rem(seg + 1, S), grp, rep))

    def section(first, last):
        total = jnp.zeros((rows, CHUNK), f32)
        for c in range(R * chunks):
            if first:
                x = embed_ref[pl.ds(pl.multiple_of(block * rows, rows), rows), c * CHUNK : (c + 1) * CHUNK]
                x_buf[c] = x
            else:
                x_arrival(c).wait_recv()
                x = x_buf[c]
            x = x.astype(f32)
            total = total + x * x
        scale = lax.rsqrt(jnp.sum(total, axis=-1, keepdims=True) / width + EPSILON)
        for c in range(R * chunks):
            cols = slice(c * CHUNK, (c + 1) * CHUNK)
            normed[:, cols] = (x_buf[c].astype(f32) * scale * gain_ref[:, cols]).astype(bf16)

        def one(j, carry):
            weight_copy(j).wait()
            update = dot(normed[...], weight[j])
            out_buf[j] = (x_buf[rep * chunks + j].astype(f32) + update).astype(bf16)
            for to in range(R):
                if last is None:
                    x_copy(j, to).start()
                else:

                    @pl.when(jnp.logical_not(last))
                    def _():
                        x_copy(j, to).start()

            return carry

        lax.fori_loop(0, chunks, one, 0)

    def drain_sends():
        def one(j, carry):
            for to in range(R):
                x_copy(j, to).wait_send()
            return carry

        lax.fori_loop(0, chunks, one, 0)

    @pl.when(seg == 0)
    def _():
        section(True, None)

    features = pl.ds(pl.multiple_of(grp * depth, depth), depth)
    table = embed_ref[...].astype(f32)
    square = jnp.sum(table * table, axis=-1, keepdims=True)
    unit_scale = lax.rsqrt(square / width + EPSILON)
    own_table = embed_ref[:, features]
    up = up_ref[...]
    unit_own = (own_table.astype(f32) * unit_scale).astype(bf16)
    part[:, 0:vr, :] = dot(own_table, up).reshape(teams, vr, rank)
    head_own = head_ref[features, :].astype(f32).T * final_gain_ref[:, features]
    high, low = halves(head_own)
    part[:, vr : 2 * vr, :] = (dot(high, up) + dot(low, up)).reshape(teams, vr, rank)
    part[:, 2 * vr : 3 * vr, :] = dot(unit_own, down_ref[...]).reshape(teams, vr, rank)
    part[:, 3 * vr :, :] = dot(up, up, ((0,), (0,))).reshape(teams, rr, rank)

    z_copies = [
        remote(
            part.at[team], from_z.at[b - 1], z_send.at[b - 1], z_recv.at[b - 1], (seg, lax.rem(grp + b, G), rep)
        )
        for b in range(1, G)
    ]
    for copy in z_copies:
        copy.start()

    def owner(g):
        return (seg * G + g) // S

    def share_row(g):
        flat = (seg * G + g) * R + rep
        return pl.multiple_of((flat - owner(g) * teams) * share, share)

    def up_copy(b):
        target = lax.rem(grp + b, G)
        return remote(
            up_ref.at[pl.ds(share_row(target), share), :],
            up_share,
            u_send.at[b - 1],
            u_recv.at[0],
            (seg, target, rep),
        )

    for b in range(1, G):

        @pl.when(owner(lax.rem(grp + b, G)) == grp)
        def _():
            up_copy(b).start()

    @pl.when(owner(grp) == grp)
    def _():
        up_share[...] = up_ref[pl.ds(share_row(grp), share), :]

    @pl.when(owner(grp) != grp)
    def _():
        remote(up_share, up_share, u_send.at[0], u_recv.at[0], (seg, lax.rem(grp + 1, G), rep)).wait_recv()

    for copy in z_copies:
        copy.wait_recv()
    total = part[team]
    for b in range(1, G):
        total = total + from_z[b - 1]
    gathered[team] = total
    g_copies = []
    for a in range(S):
        for c in range(R):
            if a + c:
                k = a * R + c - 1
                g_copies.append(
                    remote(
                        gathered.at[team],
                        gathered.at[team],
                        g_send.at[k],
                        g_recv.at[k],
                        (lax.rem(seg + a, S), grp, lax.rem(rep + c, R)),
                    )
                )
    for copy in g_copies:
        copy.start()

    @pl.when(seg == 1)
    def _():
        section(False, None)

    for copy in token_copies:
        copy.wait_recv()
    ids_iota = lax.broadcasted_iota(jnp.int32, (vocab, tokens.shape[2]), 0)

    def count(g, carry):
        for i in range(group_seqs):
            here = (tokens[g, i : i + 1, :] == ids_iota).astype(bf16)
            there = (tokens[g, group_seqs + i : group_seqs + i + 1, :] == ids_iota).astype(bf16)
            pair_count[g * group_seqs + i] = dot(here, there, ((1,), (1,)))
        return carry

    lax.fori_loop(0, G, count, 0)

    table_gain = embed_ref[...].astype(f32) * final_gain_ref[...]
    high, low = halves(table_gain)
    table_logits = dot(high, head_ref[...]) + dot(low, head_ref[...])
    for copy in g_copies:
        copy.wait_recv()
    table_up = gathered[:, 0:vr, :].reshape(vocab, rank)
    head_up = gathered[:, vr : 2 * vr, :].reshape(vocab, rank)
    latent = gathered[:, 2 * vr : 3 * vr, :].reshape(vocab, rank).astype(bf16)
    up_up = gathered[:, 3 * vr :, :].reshape(rank, rank)
    lat_buf[...] = latent
    latent_wide = latent.astype(f32)
    lat_up = exact(latent_wide, up_up)
    hidden_square = square + jnp.sum(latent_wide * (2.0 * table_up + lat_up), axis=-1, keepdims=True)
    inverse = lax.rsqrt(hidden_square / width + EPSILON)
    raw_logits = table_logits + exact(latent_wide, head_up, ((1,), (1,)))
    agent_logp = log_softmax(inverse * raw_logits)
    rank_buf[0] = head_up
    rank_buf[1] = table_up + lat_up
    wide_buf[0] = jnp.broadcast_to(inverse, (vocab, vocab))
    wide_buf[1] = raw_logits
    wide_buf[2] = jnp.exp(agent_logp)
    hidden_share[...] = embed_share_ref[...].astype(f32) + dot(latent, up_share[...], ((1,), (1,)))
    wide_buf[3] = agent_logp

    def agent_term(g, carry):
        first = pl.multiple_of(g * group_seqs, group_seqs)
        agent_terms[pl.ds(first, group_seqs), :] = jnp.sum(
            pair_count[pl.ds(first, group_seqs)] * wide_buf[3][None], axis=1
        )
        return carry

    lax.fori_loop(0, G, agent_term, 0)

    @pl.when(seg >= 2)
    def _():
        section(False, seg == S - 1)

    def term_copy(a, b):
        target = cohort * blocks + lax.rem(block + b, blocks)
        k = a * blocks + b - 1
        return remote(
            terms.at[block], terms.at[block], t_send.at[k], t_recv.at[b], (lax.rem(seg + a, S), target, rep)
        )

    @pl.when(seg == S - 1)
    def _():
        logits = jnp.zeros((rows, vocab), f32)
        squares = jnp.zeros((rows, CHUNK), f32)
        for j in range(chunks):
            cols = pl.ds(pl.multiple_of((rep * chunks + j) * CHUNK, CHUNK), CHUNK)
            x = out_buf[j].astype(f32)
            squares = squares + x * x
            logits = logits + dot((x * final_gain_ref[:, cols]).astype(bf16), head_ref[cols, :])
        exchange[0, 0] = logits
        exchange[0, 1] = jnp.broadcast_to(jnp.sum(squares, axis=-1, keepdims=True), (rows, vocab))
        e_copies = [
            remote(exchange.at[0], exchange.at[c], e_send.at[c - 1], e_recv.at[c - 1], (seg, grp, lax.rem(rep + c, R)))
            for c in range(1, R)
        ]
        for copy in e_copies:
            copy.start()
        for copy in e_copies:
            copy.wait_recv()
        logits = exchange[0, 0]
        squares = exchange[0, 1]
        for c in range(1, R):
            logits = logits + exchange[c, 0]
            squares = squares + exchange[c, 1]
        exchange_logp = log_softmax(logits * lax.rsqrt(squares / width + EPSILON))
        exchange[R, 0] = exchange_logp
        own_rows = pl.ds(pl.multiple_of(block * rows, rows), rows)

        def prior_term(g, carry):
            first = pl.multiple_of(g * group_seqs, group_seqs)
            terms[block, pl.ds(first, group_seqs), :] = jnp.sum(
                pair_count[pl.ds(first, group_seqs), own_rows, :] * exchange[R, 0][None], axis=1
            )
            return carry

        lax.fori_loop(0, G, prior_term, 0)
        for a in range(S):
            for b in range(blocks):
                if a + b:
                    term_copy(a, b).start()
        for copy in e_copies:
            copy.wait_send()

    for b in range(blocks):

        def wait_term():
            came = lax.rem(block + blocks - b, blocks)
            remote(
                terms.at[came], terms.at[came], t_send.at[0], t_recv.at[b], (lax.rem(seg + 1, S), grp, rep)
            ).wait_recv()

        if b == 0:
            pl.when(seg != S - 1)(wait_term)
        else:
            wait_term()

    difference = -agent_terms[...]
    for b in range(blocks):
        difference = difference + terms[b]
    counts = tokens[:, 2 * group_seqs : 3 * group_seqs, :].reshape(seqs, -1).astype(f32)
    scores = tokens[:, 3 * group_seqs :, :].reshape(seqs, -1).astype(f32)
    margin = jnp.sum(difference, axis=-1, keepdims=True) / counts + SIGMA_WEIGHT * scores / LEVELS
    factor_buf[...] = 2.0 * margin / counts

    def weigh(i, total):
        for k in range(4):
            total = total + pair_count[i * 4 + k] * factor_buf[pl.ds(i * 4 + k, 1), :]
        return total

    weighted = lax.fori_loop(0, seqs // 4, weigh, jnp.zeros((vocab, vocab), f32))
    logit_grad = jnp.sum(weighted, axis=-1, keepdims=True) * wide_buf[2] - weighted
    inverse = wide_buf[0][:, 0:1]
    mean = jnp.sum(logit_grad * wide_buf[1], axis=-1, keepdims=True) / width
    pull = inverse * inverse * inverse * mean
    latent_grad = (inverse * exact(logit_grad, rank_buf[0]) - pull * rank_buf[1]).astype(bf16)
    wide_share = embed_share_ref[...].astype(f32)
    table = embed_ref[...].astype(f32)
    unit_scale = lax.rsqrt(jnp.sum(table * table, axis=-1, keepdims=True) / width + EPSILON)
    unit_share = (wide_share * unit_scale).astype(bf16)
    down_out[...] = dot(unit_share, latent_grad, ((0,), (0,)))
    scaled = dot(logit_grad.astype(bf16), head_share_ref[...], ((1,), (1,))) * gain_share_ref[...]
    hidden_grad = (inverse * scaled - hidden_share[...] * pull).astype(bf16)
    up_out[...] = dot(hidden_grad, lat_buf[...], ((0,), (0,)))

    for copy in token_copies + z_copies + g_copies:
        copy.wait_send()
    for b in range(1, G):

        @pl.when(owner(lax.rem(grp + b, G)) == grp)
        def _():
            up_copy(b).wait_send()

    @pl.when(seg != S - 1)
    def _():
        drain_sends()

    @pl.when(seg == S - 1)
    def _():
        for a in range(S):
            for b in range(blocks):
                if a + b:
                    term_copy(a, b).wait_send()


def on_device(
    token_ids,
    seq_lengths,
    quant_scores,
    embed_table,
    prior_weight,
    prior_gain,
    final_gain,
    head_weight,
    agent_down,
    agent_up,
):
    S, G, R = (lax.axis_size(a) for a in ("segment", "fsdp", "rep"))
    seg, grp, rep = (lax.axis_index(a) for a in ("segment", "fsdp", "rep"))
    vocab, width = embed_table.shape
    rank = agent_up.shape[1]
    group_seqs, seq_len = token_ids.shape
    seqs = group_seqs * G
    half = prior_weight.shape[2]
    chunks = half // CHUNK
    rows = max(16, vocab // G)
    blocks = vocab // rows
    teams = S * R
    vr, rr = vocab // teams, rank // teams
    share = width // (S * G * R)

    positions = jnp.arange(seq_len, dtype=jnp.int32)
    ahead = jnp.concatenate([token_ids[:, 1:], token_ids[:, :1]], axis=1)
    spread = lambda v: jnp.broadcast_to(v[:, None], (group_seqs, seq_len))
    pack = jnp.concatenate(
        [
            token_ids,
            jnp.where(positions[None, :] < seq_lengths[:, None] - 1, ahead, -1),
            spread(seq_lengths - 1),
            spread(quant_scores),
        ],
        axis=0,
    )
    first = ((seg * G + grp) * R + rep) * share
    embed_share = lax.dynamic_slice_in_dim(embed_table, first, share, 1)
    head_share = lax.dynamic_slice_in_dim(head_weight, first, share, 0)
    gain_share = lax.dynamic_slice_in_dim(final_gain, first, share, 0)[None]

    vmem = pl.BlockSpec(memory_space=pltpu.VMEM)
    dma = pltpu.SemaphoreType.DMA
    return pl.pallas_call(
        functools.partial(kernel, (S, G, R)),
        out_shape=[jax.ShapeDtypeStruct((share, rank), f32)] * 2,
        in_specs=[vmem] * 10 + [pl.BlockSpec(memory_space=pl.ANY)],
        out_specs=[vmem, vmem],
        scratch_shapes=[
            pltpu.VMEM((chunks, width, CHUNK), bf16),
            pltpu.VMEM((R * chunks, rows, CHUNK), bf16),
            pltpu.VMEM((rows, width), bf16),
            pltpu.VMEM((chunks, rows, CHUNK), bf16),
            pltpu.VMEM((G, 4 * group_seqs, seq_len), jnp.int32),
            pltpu.VMEM((teams, 3 * vr + rr, rank), f32),
            pltpu.VMEM((G - 1, 3 * vr + rr, rank), f32),
            pltpu.VMEM((teams, 3 * vr + rr, rank), f32),
            pltpu.VMEM((share, rank), bf16),
            pltpu.VMEM((seqs, vocab, vocab), f32),
            pltpu.VMEM((R + 1, 2, rows, vocab), f32),
            pltpu.VMEM((blocks, seqs, vocab), f32),
            pltpu.VMEM((seqs, vocab), f32),
            pltpu.VMEM((vocab, rank), bf16),
            pltpu.VMEM((4, vocab, vocab), f32),
            pltpu.VMEM((2, vocab, rank), f32),
            pltpu.VMEM((seqs, vocab), f32),
            pltpu.VMEM((vocab, share), f32),
            dma((chunks,)),
            dma((chunks, R)),
            dma((R * chunks,)),
            dma((G - 1,)),
            dma((G - 1,)),
            dma((G - 1,)),
            dma((G - 1,)),
            dma((teams - 1,)),
            dma((teams - 1,)),
            dma((G - 1,)),
            dma((1,)),
            dma((R - 1,)),
            dma((R - 1,)),
            dma((S * blocks - 1,)),
            dma((blocks,)),
        ],
        compiler_params=pltpu.CompilerParams(
            collective_id=0, has_side_effects=True, vmem_limit_bytes=56 * 1024 * 1024
        ),
    )(
        pack,
        embed_table,
        prior_gain,
        final_gain[None],
        head_weight,
        agent_down,
        agent_up,
        embed_share,
        head_share,
        gain_share,
        prior_weight,
    )


def solution(mesh):
    placed = (
        P("fsdp", None),
        P("fsdp"),
        P("fsdp"),
        P(),
        P("segment", None, "rep"),
        P("segment", None),
        P(),
        P(),
        P("fsdp", None),
        P("fsdp", None),
    )
    spread = P(("segment", "fsdp", "rep"), None)

    def run(*args):
        return tuple(on_device(*args))

    return jax.shard_map(run, mesh=mesh, in_specs=placed, out_specs=(spread, spread), check_vma=False)
```

time: 227 us -> 70.4 us (0.31)
  waiting for transfers between devices: 107 us -> 0 us
  Pallas kernels: 0 us -> 59.1 us
  matrix products: 51 us -> 0 us
  blocking collectives: 29.7 us -> 0 us
  between operations: 16.5 us -> 0.65 us
  starting transfers between devices: 14.3 us -> 0 us
  local copies, waits for them, and re-layouts: 3.38 us -> 7.44 us
    psum x1 -> x0, waiting for transfers between devices: 95.5 us -> none  [on_device(): prior_logp = lax.psum(slot, ('segment', 'fsdp'))]
    pallas_call x0 -> x1, Pallas kernels: none -> 59.1 us  [on_device(): pl.pallas_call(functools.partial(kernel, (S, G, R)), out_shape=[jax.Shape...]
    dot_general x15 -> x0, matrix products: 51 us -> none  [dot(): return lax.dot_general(a, b, (dims, ((), ())), preferred_element_type=f32)]
    all_gather x5 -> x0, blocking collectives: 21.7 us -> none  [the longest x1 13.4 us: on_device(): ids = lax.all_gather(token_ids, 'fsdp', axis=0, tiled=True)]
    ppermute x3 -> x0, starting transfers between devices: 14.2 us -> none  [on_device(): rows = lax.ppermute(rows, 'segment', pairs)]
    ppermute x3 -> x0, waiting for transfers between devices: 11 us -> none  [on_device(): rows = lax.ppermute(rows, 'segment', pairs)]
    unnamed x1 -> x0, blocking collectives: 7.98 us -> none
    reduce_sum x9 -> x0, other arithmetic: 2.41 us -> none  [the longest x6 2.07 us: rms_scale(): squares = jnp.mean(values * values, axis=-1, keepdims=True)]
  transfers between devices with their start and end apart: 6 -> 0, of which waited for: 3 -> 0; matrix products, arithmetic and copies ran while one was open for 21% -> 0% of each run, Pallas kernels for 0% -> 0%
where the time goes in v1:
time: 70.4 us; the launch traced here: 70 us
  Pallas kernels  59.1 us (84%)
  local copies, waits for them, and re-layouts  7.44 us (11%)
  other arithmetic  2.78 us (4%)
    pallas_call x1, Pallas kernels, on_device(): pl.pallas_call(functools.partial(kernel, (S, G, R)), out_shape=[jax.Shape...  59.1 us
    unnamed x2, local copies, waits for them, and re-layouts  3.14 us

profile of v1, /device:TPU:0, one launch (start us, length us, event | category | flops | bytes accessed | tf_op | source)
XLA Modules:
  0.0 70.0 jit_solution(14060587251728758265)
XLA Ops:
  0.6 0.7 broadcast_add_fusion
  1.3 0.7 %pad.3.clone = s32[32]{0:T(128)S(1)} pad(s32[8]{0:T(128)} %param.12, s32[]{:T(128)} %constant.9.clone.1), padding=24_0 | pad | bytes 164 | tf_op jit(solution)/shard_map/concatenate | solution.py:466
  2.0 1.3 %dynamic-slice_bitcast_fusion.gain_share_ref = f32[1,128]{1,0:T(1,128)} fusion(f32[4096]{0:T(1024)} %param.16, s32[]{:T(128)S(6)} %select_n.10), kind=kLoop, calls=%fused_computation.3 | loop fusion | bytes 1028 | tf_op jit(solution)/shard_map/broadcast_in_dim | solution.py:478
  3.4 0.1 lt.9
  3.4 0.8 %slice.6 = s32[8,127]{1,0:T(8,128)S(1)} slice(s32[8,128]{1,0:T(8,128)} %param.10), slice={[0:8], [1:128]} | slice | bytes 8128 | tf_op jit(solution)/shard_map/slice | solution.py:464
  4.2 0.8 %add_select_fusion = s32[8,128]{1,0:T(8,128)S(1)} fusion(s32[8,1]{1,0:T(8,128)} %bitcast.4, s32[8,127]{1,0:T(8,128)S(1)} %slice.6, s32[8]{0:T(128)S(1)} %broadcast_add_fusion), kind=kLoop, calls=%fused_computation.1 | loop fusion | flops 3072 | bytes 8224 | tf_op jit(solution)/shard_map/jit(_where)/select_n | solution.py:469
  5.0 1.4 %add_add_fusion.pack_ref = s32[32,128]{1,0:T(8,128)} fusion(s32[8,128]{1,0:T(8,128)S(1)} %lt.9, s32[8,128]{1,0:T(8,128)S(1)} %add_select_fusion, s32[8,128]{1,0:T(8,128)} %param.10, s32[32]{0:T(128)S(1)} %pad.3.clone), kind=kLoop, calls=%fused_computation | loop fusion | flops 12288 | bytes 28800 | tf_op jit(solution)/shard_map/concatenate | solution.py:466
  6.3 1.4 %constant_dynamic-slice_fusion = (bf16[128,128]{1,0:T(8,128)(2,1)}, bf16[128,128]{1,0:T(8,128)(2,1)}) fusion(bf16[4096,128]{1,0:T(8,128)(2,1)} %head_ref.1, s32[]{:T(128)S(6)} %select_n.10, bf16[128,4096]{1,0:T(8,128)(2,1)} %embed_ref.1), kind=kLoop, calls=%fused_computation.4 | loop fusion | bytes 131076 | tf_op jit(solution)/shard_map/dynamic_slice | solution.py:477
  7.7 59.1 %shard_map.113 = (f32[128,256]{1,0:T(8,128)}, f32[128,256]{1,0:T(8,128)}) custom-call(s32[32,128]{1,0:T(8,128)} %add_add_fusion.pack_ref, bf16[128,4096]{1,0:T(8,128)(2,1)} %embed_ref.1, f32[1,4096]{1,0:T(1,128)} %gain_ref.1, f32[1,4096]{1,0:T(1,128)} %bitcast.5, bf16[4096,128]{1,0:T(8,128)(2,1)} %head_ref.1, bf16[1024,256]{1,0:T(8,128)(2,1)} %down_ref.1, ...), custom_call_target="tpu_custom_call" | custom-call | tf_op jit(solution)/shard_map/pallas_call | solution.py:482
  66.9 1.6 %copy.14 = f32[128,256]{1,0:T(8,128)} copy(f32[128,256]{1,0:T(8,128)} %get-tuple-element.6) | data formatting | bytes 262144
  68.4 1.6 %copy.15 = f32[128,256]{1,0:T(8,128)} copy(f32[128,256]{1,0:T(8,128)} %get-tuple-element.7) | data formatting | bytes 262144

commit v2 on v1

--- a/solution.py
+++ b/solution.py
@@ -37,16 +37,15 @@
 
 def kernel(
     sizes,
-    pack_ref,
+    ids_ref,
+    length_ref,
+    score_ref,
     embed_ref,
     gain_ref,
     final_gain_ref,
     head_ref,
     down_ref,
     up_ref,
-    embed_share_ref,
-    head_share_ref,
-    gain_share_ref,
     weight_hbm,
     down_out,
     up_out,
@@ -65,7 +64,10 @@
     factor_buf,
     lat_buf,
     wide_buf,
+    head_up_buf,
     rank_buf,
+    pack_ref,
+    window_out,
     agent_terms,
     hidden_share,
     weight_sem,
@@ -97,7 +99,11 @@
     teams = S * R
     team = seg * R + rep
     vr, rr = vocab // teams, rank // teams
-    share = up_share.shape[0]
+    share = down_out.shape[0]
+    window = up_share.shape[0]
+    first = ((seg * G + grp) * R + rep) * share
+    base = pl.multiple_of(first - lax.rem(first, window), window)
+    window_cols = pl.ds(base, window)
     seqs = pair_count.shape[0]
     group_seqs = seqs // G
 
@@ -123,41 +129,41 @@
                 if a + b + c:
                     other = (lax.rem(seg + a, S), lax.rem(grp + b, G), lax.rem(rep + c, R))
                     pl.semaphore_signal(barrier, inc=1, device_id=other, device_id_type=MESH)
-    pl.semaphore_wait(barrier, S * G * R - 1)
-
-    tokens[grp] = pack_ref[...]
-    token_copies = [
-        remote(
-            pack_ref, tokens.at[grp], tok_send.at[b - 1], tok_recv.at[b - 1], (seg, lax.rem(grp + b, G), rep)
-        )
-        for b in range(1, G)
-    ]
-    for copy in token_copies:
-        copy.start()
-
-    def x_copy(j, to):
+
+    def x_copy(j):
+        c = rep * chunks + j
+        return remote(out_buf.at[j], x_buf.at[c], x_send.at[j, 0], x_recv.at[c], (lax.rem(seg + 1, S), grp, rep))
+
+    def x_arrival(c):
         return remote(
-            out_buf.at[j],
-            x_buf.at[rep * chunks + j],
-            x_send.at[j, to],
-            x_recv.at[rep * chunks + j],
-            (lax.rem(seg + 1, S), grp, to),
-        )
-
-    def x_arrival(c):
-        return remote(out_buf.at[0], x_buf.at[c], x_send.at[0, 0], x_recv.at[c], (lax.rem(seg + 1, S), grp, rep))
+            out_buf.at[0], x_buf.at[c], x_send.at[0, 0], x_recv.at[c], (lax.rem(seg + 1, S), grp, rep)
+        )
+
+    def x_forward(j, k):
+        c = rep * chunks + j
+        return remote(x_buf.at[c], x_buf.at[c], x_send.at[j, k], x_recv.at[c], (seg, grp, lax.rem(rep + k, R)))
 
     def section(first, last):
         total = jnp.zeros((rows, CHUNK), f32)
-        for c in range(R * chunks):
-            if first:
+        if first:
+            for c in range(R * chunks):
                 x = embed_ref[pl.ds(pl.multiple_of(block * rows, rows), rows), c * CHUNK : (c + 1) * CHUNK]
                 x_buf[c] = x
-            else:
-                x_arrival(c).wait_recv()
-                x = x_buf[c]
-            x = x.astype(f32)
-            total = total + x * x
+                x = x.astype(f32)
+                total = total + x * x
+        else:
+            for j in range(chunks):
+                x_arrival(rep * chunks + j).wait_recv()
+                for k in range(1, R):
+                    x_forward(j, k).start()
+                x = x_buf[rep * chunks + j].astype(f32)
+                total = total + x * x
+            for j in range(chunks):
+                for k in range(1, R):
+                    c = lax.rem(rep + k, R) * chunks + j
+                    x_arrival(c).wait_recv()
+                    x = x_buf[c].astype(f32)
+                    total = total + x * x
         scale = lax.rsqrt(jnp.sum(total, axis=-1, keepdims=True) / width + EPSILON)
         for c in range(R * chunks):
             cols = slice(c * CHUNK, (c + 1) * CHUNK)
@@ -167,30 +173,25 @@
             weight_copy(j).wait()
             update = dot(normed[...], weight[j])
             out_buf[j] = (x_buf[rep * chunks + j].astype(f32) + update).astype(bf16)
-            for to in range(R):
-                if last is None:
-                    x_copy(j, to).start()
-                else:
-
-                    @pl.when(jnp.logical_not(last))
-                    def _():
-                        x_copy(j, to).start()
+            if last is None:
+                x_copy(j).start()
+            else:
+
+                @pl.when(jnp.logical_not(last))
+                def _():
+                    x_copy(j).start()
 
             return carry
 
         lax.fori_loop(0, chunks, one, 0)
 
-    def drain_sends():
+    def drain(copies):
         def one(j, carry):
-            for to in range(R):
-                x_copy(j, to).wait_send()
+            for copy in copies(j):
+                copy.wait_send()
             return carry
 
         lax.fori_loop(0, chunks, one, 0)
-
-    @pl.when(seg == 0)
-    def _():
-        section(True, None)
 
     features = pl.ds(pl.multiple_of(grp * depth, depth), depth)
     table = embed_ref[...].astype(f32)
@@ -206,6 +207,29 @@
     part[:, 2 * vr : 3 * vr, :] = dot(unit_own, down_ref[...]).reshape(teams, vr, rank)
     part[:, 3 * vr :, :] = dot(up, up, ((0,), (0,))).reshape(teams, rr, rank)
 
+    pl.semaphore_wait(barrier, S * G * R - 1)
+    position = lax.broadcasted_iota(jnp.int32, (1, ids_ref.shape[1]), 1)
+    ids = ids_ref[...]
+    pack_ref[0:group_seqs, :] = ids
+    ahead = pltpu.roll(ids, ids.shape[1] - 1, 1)
+    for i in range(group_seqs):
+        count_now = length_ref[i] - 1
+        at = group_seqs + i
+        pack_ref[at : at + 1, :] = jnp.where(position < count_now, ahead[i : i + 1, :], -1)
+        at = at + group_seqs
+        pack_ref[at : at + 1, :] = jnp.zeros_like(position) + count_now
+        at = at + group_seqs
+        pack_ref[at : at + 1, :] = jnp.zeros_like(position) + score_ref[i]
+    tokens[grp] = pack_ref[...]
+    token_copies = [
+        remote(
+            pack_ref, tokens.at[grp], tok_send.at[b - 1], tok_recv.at[b - 1], (seg, lax.rem(grp + b, G), rep)
+        )
+        for b in range(1, G)
+    ]
+    for copy in token_copies:
+        copy.start()
+
     z_copies = [
         remote(
             part.at[team], from_z.at[b - 1], z_send.at[b - 1], z_recv.at[b - 1], (seg, lax.rem(grp + b, G), rep)
@@ -220,12 +244,13 @@
 
     def share_row(g):
         flat = (seg * G + g) * R + rep
-        return pl.multiple_of((flat - owner(g) * teams) * share, share)
+        row = (flat - owner(g) * teams) * share
+        return pl.multiple_of(row - lax.rem(row, window), window)
 
     def up_copy(b):
         target = lax.rem(grp + b, G)
         return remote(
-            up_ref.at[pl.ds(share_row(target), share), :],
+            up_ref.at[pl.ds(share_row(target), window), :],
             up_share,
             u_send.at[b - 1],
             u_recv.at[0],
@@ -240,18 +265,22 @@
 
     @pl.when(owner(grp) == grp)
     def _():
-        up_share[...] = up_ref[pl.ds(share_row(grp), share), :]
+        up_share[...] = up_ref[pl.ds(share_row(grp), window), :]
 
     @pl.when(owner(grp) != grp)
     def _():
         remote(up_share, up_share, u_send.at[0], u_recv.at[0], (seg, lax.rem(grp + 1, G), rep)).wait_recv()
+
+    @pl.when(seg == 0)
+    def _():
+        section(True, None)
 
     for copy in z_copies:
         copy.wait_recv()
     total = part[team]
     for b in range(1, G):
         total = total + from_z[b - 1]
-    gathered[team] = total
+    gathered[team] = total.astype(bf16)
     g_copies = []
     for a in range(S):
         for c in range(R):
@@ -291,23 +320,23 @@
     table_logits = dot(high, head_ref[...]) + dot(low, head_ref[...])
     for copy in g_copies:
         copy.wait_recv()
-    table_up = gathered[:, 0:vr, :].reshape(vocab, rank)
+    table_up = gathered[:, 0:vr, :].reshape(vocab, rank).astype(f32)
     head_up = gathered[:, vr : 2 * vr, :].reshape(vocab, rank)
-    latent = gathered[:, 2 * vr : 3 * vr, :].reshape(vocab, rank).astype(bf16)
+    latent = gathered[:, 2 * vr : 3 * vr, :].reshape(vocab, rank)
     up_up = gathered[:, 3 * vr :, :].reshape(rank, rank)
     lat_buf[...] = latent
     latent_wide = latent.astype(f32)
-    lat_up = exact(latent_wide, up_up)
+    lat_up = dot(latent, up_up)
     hidden_square = square + jnp.sum(latent_wide * (2.0 * table_up + lat_up), axis=-1, keepdims=True)
     inverse = lax.rsqrt(hidden_square / width + EPSILON)
-    raw_logits = table_logits + exact(latent_wide, head_up, ((1,), (1,)))
+    raw_logits = table_logits + dot(latent, head_up, ((1,), (1,)))
     agent_logp = log_softmax(inverse * raw_logits)
-    rank_buf[0] = head_up
-    rank_buf[1] = table_up + lat_up
+    head_up_buf[...] = head_up
+    rank_buf[...] = table_up + lat_up
     wide_buf[0] = jnp.broadcast_to(inverse, (vocab, vocab))
     wide_buf[1] = raw_logits
     wide_buf[2] = jnp.exp(agent_logp)
-    hidden_share[...] = embed_share_ref[...].astype(f32) + dot(latent, up_share[...], ((1,), (1,)))
+    hidden_share[...] = embed_ref[:, window_cols].astype(f32) + dot(latent, up_share[...], ((1,), (1,)))
     wide_buf[3] = agent_logp
 
     def agent_term(g, carry):
@@ -404,15 +433,26 @@
     inverse = wide_buf[0][:, 0:1]
     mean = jnp.sum(logit_grad * wide_buf[1], axis=-1, keepdims=True) / width
     pull = inverse * inverse * inverse * mean
-    latent_grad = (inverse * exact(logit_grad, rank_buf[0]) - pull * rank_buf[1]).astype(bf16)
-    wide_share = embed_share_ref[...].astype(f32)
+    high, low = halves(logit_grad)
+    pulled = dot(high, head_up_buf[...]) + dot(low, head_up_buf[...])
+    latent_grad = (inverse * pulled - pull * rank_buf[...]).astype(bf16)
+    wide_share = embed_ref[:, window_cols].astype(f32)
     table = embed_ref[...].astype(f32)
     unit_scale = lax.rsqrt(jnp.sum(table * table, axis=-1, keepdims=True) / width + EPSILON)
     unit_share = (wide_share * unit_scale).astype(bf16)
-    down_out[...] = dot(unit_share, latent_grad, ((0,), (0,)))
-    scaled = dot(logit_grad.astype(bf16), head_share_ref[...], ((1,), (1,))) * gain_share_ref[...]
+    down_share = dot(unit_share, latent_grad, ((0,), (0,)))
+    scaled = dot(logit_grad.astype(bf16), head_ref[window_cols, :], ((1,), (1,))) * final_gain_ref[:, window_cols]
     hidden_grad = (inverse * scaled - hidden_share[...] * pull).astype(bf16)
-    up_out[...] = dot(hidden_grad, lat_buf[...], ((0,), (0,)))
+    up_grad = dot(hidden_grad, lat_buf[...], ((0,), (0,)))
+    if window == share:
+        down_out[...] = down_share
+        up_out[...] = up_grad
+    else:
+        window_out[0] = down_share
+        window_out[1] = up_grad
+        within = pl.ds(pl.multiple_of(first - base, share), share)
+        down_out[...] = window_out[0, within, :]
+        up_out[...] = window_out[1, within, :]
 
     for copy in token_copies + z_copies + g_copies:
         copy.wait_send()
@@ -424,7 +464,11 @@
 
     @pl.when(seg != S - 1)
     def _():
-        drain_sends()
+        drain(lambda j: [x_copy(j)])
+
+    @pl.when(seg != 0)
+    def _():
+        drain(lambda j: [x_forward(j, k) for k in range(1, R)])
 
     @pl.when(seg == S - 1)
     def _():
@@ -447,7 +491,6 @@
     agent_up,
 ):
     S, G, R = (lax.axis_size(a) for a in ("segment", "fsdp", "rep"))
-    seg, grp, rep = (lax.axis_index(a) for a in ("segment", "fsdp", "rep"))
     vocab, width = embed_table.shape
     rank = agent_up.shape[1]
     group_seqs, seq_len = token_ids.shape
@@ -459,30 +502,15 @@
     teams = S * R
     vr, rr = vocab // teams, rank // teams
     share = width // (S * G * R)
-
-    positions = jnp.arange(seq_len, dtype=jnp.int32)
-    ahead = jnp.concatenate([token_ids[:, 1:], token_ids[:, :1]], axis=1)
-    spread = lambda v: jnp.broadcast_to(v[:, None], (group_seqs, seq_len))
-    pack = jnp.concatenate(
-        [
-            token_ids,
-            jnp.where(positions[None, :] < seq_lengths[:, None] - 1, ahead, -1),
-            spread(seq_lengths - 1),
-            spread(quant_scores),
-        ],
-        axis=0,
-    )
-    first = ((seg * G + grp) * R + rep) * share
-    embed_share = lax.dynamic_slice_in_dim(embed_table, first, share, 1)
-    head_share = lax.dynamic_slice_in_dim(head_weight, first, share, 0)
-    gain_share = lax.dynamic_slice_in_dim(final_gain, first, share, 0)[None]
-
+    window = max(share, 128)
+
+    smem = pl.BlockSpec(memory_space=pltpu.SMEM)
     vmem = pl.BlockSpec(memory_space=pltpu.VMEM)
     dma = pltpu.SemaphoreType.DMA
     return pl.pallas_call(
         functools.partial(kernel, (S, G, R)),
         out_shape=[jax.ShapeDtypeStruct((share, rank), f32)] * 2,
-        in_specs=[vmem] * 10 + [pl.BlockSpec(memory_space=pl.ANY)],
+        in_specs=[vmem, smem, smem] + [vmem] * 6 + [pl.BlockSpec(memory_space=pl.ANY)],
         out_specs=[vmem, vmem],
         scratch_shapes=[
             pltpu.VMEM((chunks, width, CHUNK), bf16),
@@ -492,17 +520,20 @@
             pltpu.VMEM((G, 4 * group_seqs, seq_len), jnp.int32),
             pltpu.VMEM((teams, 3 * vr + rr, rank), f32),
             pltpu.VMEM((G - 1, 3 * vr + rr, rank), f32),
-            pltpu.VMEM((teams, 3 * vr + rr, rank), f32),
-            pltpu.VMEM((share, rank), bf16),
+            pltpu.VMEM((teams, 3 * vr + rr, rank), bf16),
+            pltpu.VMEM((window, rank), bf16),
             pltpu.VMEM((seqs, vocab, vocab), f32),
             pltpu.VMEM((R + 1, 2, rows, vocab), f32),
             pltpu.VMEM((blocks, seqs, vocab), f32),
             pltpu.VMEM((seqs, vocab), f32),
             pltpu.VMEM((vocab, rank), bf16),
             pltpu.VMEM((4, vocab, vocab), f32),
-            pltpu.VMEM((2, vocab, rank), f32),
+            pltpu.VMEM((vocab, rank), bf16),
+            pltpu.VMEM((vocab, rank), f32),
+            pltpu.VMEM((4 * group_seqs, seq_len), jnp.int32),
+            pltpu.VMEM((2, window, rank), f32),
             pltpu.VMEM((seqs, vocab), f32),
-            pltpu.VMEM((vocab, share), f32),
+            pltpu.VMEM((vocab, window), f32),
             dma((chunks,)),
             dma((chunks, R)),
             dma((R * chunks,)),
@@ -523,16 +554,15 @@
             collective_id=0, has_side_effects=True, vmem_limit_bytes=56 * 1024 * 1024
         ),
     )(
-        pack,
+        token_ids,
+        seq_lengths,
+        quant_scores,
         embed_table,
         prior_gain,
         final_gain[None],
         head_weight,
         agent_down,
         agent_up,
-        embed_share,
-        head_share,
-        gain_share,
         prior_weight,
     )
 

time: 70.4 us -> 62.8 us (0.89)
  local copies, waits for them, and re-layouts: 7.44 us -> 3.14 us
  other arithmetic: 2.78 us -> 0 us
    dynamic_slice x1 -> x0, local copies, waits for them, and re-layouts: 1.4 us -> none  [on_device(): head_share = lax.dynamic_slice_in_dim(head_weight, first, share, 0)]
    concatenate x1 -> x0, other arithmetic: 1.36 us -> none  [on_device(): jnp.concatenate([token_ids, jnp.where(positions[None, :] < seq_lengths[:,...]
    broadcast_in_dim x1 -> x0, local copies, waits for them, and re-layouts: 1.35 us -> none  [on_device(): gain_share = lax.dynamic_slice_in_dim(final_gain, first, share, 0)[None]]
    select_n x1 -> x0, other arithmetic: 0.76 us -> none  [on_device(): jnp.where(positions[None, :] < seq_lengths[:, None] - 1, ahead, -1)]
    slice x1 -> x0, local copies, waits for them, and re-layouts: 0.76 us -> none  [on_device(): ahead = jnp.concatenate([token_ids[:, 1:], token_ids[:, :1]], axis=1)]
    concatenate x1 -> x0, local copies, waits for them, and re-layouts: 0.73 us -> none  [on_device(): jnp.concatenate([token_ids, jnp.where(positions[None, :] < seq_lengths[:,...]
where the time goes in v2:
time: 62.8 us; the launch traced here: 62.6 us
  Pallas kernels  58.9 us (94%)
  local copies, waits for them, and re-layouts  3.14 us (5%)
  between operations  0.64 us (1%)
    pallas_call x1, Pallas kernels, on_device(): pl.pallas_call(functools.partial(kernel, (S, G, R)), out_shape=[jax.Shape...  58.9 us
    unnamed x2, local copies, waits for them, and re-layouts  3.14 us

profile of v2, /device:TPU:0, one launch (start us, length us, event | category | flops | bytes accessed | tf_op | source)
XLA Modules:
  0.0 62.6 jit_solution(17029281974830215486)
XLA Ops:
  0.6 58.9 %shard_map.113 = (f32[128,256]{1,0:T(8,128)}, f32[128,256]{1,0:T(8,128)}) custom-call(s32[8,128]{1,0:T(8,128)} %ids_ref.1, s32[8]{0:T(128)} %length_ref.1, s32[8]{0:T(128)} %score_ref.1, bf16[128,4096]{1,0:T(8,128)(2,1)} %embed_ref.1, f32[1,4096]{1,0:T(1,128)} %gain_ref.1, f32[1,4096]{1,0:T(1,128)} %bitcast.1, bf16[4096,128]{1,0:T(8,128)(2,1)} %head_ref.1, ...), custom_call_target="tpu_custom_call" | custom-call | tf_op jit(solution)/shard_map/pallas_call | solution.py:510
  59.5 1.6 %copy.14 = f32[128,256]{1,0:T(8,128)} copy(f32[128,256]{1,0:T(8,128)} %get-tuple-element.4) | data formatting | bytes 262144
  61.1 1.6 %copy.15 = f32[128,256]{1,0:T(8,128)} copy(f32[128,256]{1,0:T(8,128)} %get-tuple-element.5) | data formatting | bytes 262144
